TPU v7x, 32 devices: a whole 2x2x4 slice. The times are simulated.
32 devices in a mesh: dp: 2 (over y), dom: 4 (over z), tensor: 4 (over x, core).
Axes of the slice: x: 2, y: 2, z: 4, core: 2. Of those that a mesh axis runs over, the one named last changes fastest.
Arguments:
- states: bfloat16 [2, 2048, 512], P('dp', 'dom'), may hold values from -60 to 60, as said below
- w_query: bfloat16 [512, 512], P(None, 'tensor'), as said below
- w_key: bfloat16 [512, 512], P(None, 'tensor'), as said below
- w_value: bfloat16 [512, 512], P(None, 'tensor'), may hold values from -0.25 to 0.25
- w_out: bfloat16 [512, 512], P('tensor'), may hold values from -0.25 to 0.25
- send_blocks: int32 [4, 4, 2], P('dom'), may hold values from 0 to 3
- neighbor_blocks: int32 [16, 3], P('dom'), may hold values from 0 to 11, as said below
- cotangent: bfloat16 [2, 2048, 512], P('dp', 'dom'), may hold values from -6 to 6
Outputs:
- update: bfloat16 [2, 2048, 512], P('dp', 'dom', 'tensor')
- branch_grad: bfloat16 [2, 2048, 512], P('dp', 'dom', 'tensor')
- grad_query: float32 [512, 512], P(None, 'tensor')
- grad_key: float32 [512, 512], P(None, 'tensor')
- grad_value: float32 [512, 512], P(None, 'tensor')
- grad_out: float32 [512, 512], P('tensor')
Inputs may be any that keep to these rules, and one draw needn't show every extreme that they name: `neighbor_blocks`: entries index the pool of the row's own partition; every pool entry from 4 on is named by some row of that partition. `states`: real entries. `w_query`: real entries. `w_key`: real entries.
All inputs are finite; a program needn't handle non-finite values.
Results may differ from a plain program's by a relative error of at most 0.02.
The roundings to bfloat16 on the way count: a program that leaves them out, or rounds other values in their place, can miss the bound.
Values may be sent and summed in bfloat16 or wider, within the bound.
No kernel may reach another device: no remote copies, remote signals or barrier semaphores. Data moves between devices by JAX's collectives and lax.ppermute only.
A program may use at most 64 MiB of HBM per device.

v0:
```python
import math

import jax
import jax.numpy as jnp
from jax import lax
from jax.sharding import PartitionSpec as P

BLK = 128
HOPS = 2
SEND = 2
HD = 64


def shifted(block, axis, distance):
    devices = range(lax.axis_size(axis))
    route = [((i - distance) % len(devices), i) for i in devices]
    return lax.ppermute(block, axis, route)


def offset_list(hops):
    result = []
    for section in range(1, hops + 1):
        result.append(section)
        result.append(-section)
    return result


def normalize(states):
    values = states.astype(jnp.float32)
    inverse = lax.rsqrt(jnp.mean(values * values, axis=-1, keepdims=True) + 1e-05)
    return (values * inverse, inverse)


def product(form, left, right):
    return jnp.einsum(form, left, right, preferred_element_type=jnp.float32)


def attend(queries, key_pool, key_index, grad_heads, head_count):
    replicas, blocks, block_rows, widths = queries.shape
    head_size = widths // head_count
    shrink = 1.0 / math.sqrt(head_size)
    listed = key_index.shape[1]
    chosen = jnp.take(key_pool, key_index.reshape(-1), axis=1)
    chosen = chosen.reshape(replicas, blocks, listed * block_rows, 2, head_count, head_size)
    key_rows = chosen[:, :, :, 0]
    value_rows = chosen[:, :, :, 1]
    query_heads = queries.reshape(replicas, blocks, block_rows, head_count, head_size)
    grad_split = grad_heads.reshape(replicas, blocks, block_rows, head_count, head_size)
    scores = product("rbqhe,rbkhe->rbhqk", query_heads, key_rows) * shrink
    highest = jnp.max(scores, axis=-1, keepdims=True)
    powers = jnp.exp(scores - highest)
    weights = powers / jnp.sum(powers, axis=-1, keepdims=True)
    weights_low = weights.astype(jnp.bfloat16)
    mixed_rows = product("rbhqk,rbkhe->rbqhe", weights_low, value_rows).astype(jnp.bfloat16)
    prob_grad = product("rbqhe,rbkhe->rbhqk", grad_split, value_rows)
    score_grad = weights * (prob_grad - jnp.sum(weights * prob_grad, axis=-1, keepdims=True))
    score_low = (score_grad * shrink).astype(jnp.bfloat16)
    query_grad = product("rbhqk,rbkhe->rbqhe", score_low, key_rows).astype(jnp.bfloat16)
    key_grad = product("rbhqk,rbqhe->rbkhe", score_low, query_heads)
    value_grad = product("rbhqk,rbqhe->rbkhe", weights_low, grad_split)
    chosen_grad = jnp.stack([key_grad, value_grad], axis=3).reshape(
        replicas, blocks, listed, block_rows, 2 * widths
    )
    pool_size = key_pool.shape[1]
    chooser = (
        key_index[:, :, None] == jnp.arange(pool_size, dtype=jnp.int32)[None, None, :]
    ).astype(jnp.float32)
    pool_grad = jnp.einsum("bnp,rbnqc->rpqc", chooser, chosen_grad, precision=lax.Precision.HIGHEST)
    return (
        mixed_rows.reshape(replicas, blocks, block_rows, widths),
        query_grad.reshape(replicas, blocks, block_rows, widths),
        pool_grad,
    )


def body(states, w_query, w_key, w_value, w_out, send_blocks, neighbor_blocks, cotangent):
    replicas, node_count, widths = states.shape
    local_width = w_query.shape[1]
    head_count = local_width // HD
    blocks = node_count // BLK
    normed, inverse = normalize(states)
    unit_rows = normed.astype(jnp.bfloat16)
    flat_unit = unit_rows.reshape(-1, widths)
    queries = jnp.dot(flat_unit, w_query, preferred_element_type=jnp.float32).astype(jnp.bfloat16)
    queries = queries.reshape(replicas, blocks, BLK, local_width)
    paired = jnp.dot(
        flat_unit, jnp.concatenate([w_key, w_value], axis=1), preferred_element_type=jnp.float32
    ).astype(jnp.bfloat16)
    paired = paired.reshape(replicas, blocks, BLK, 2 * local_width)
    flat_cot = cotangent.reshape(-1, widths)
    grad_heads = jnp.dot(flat_cot, w_out.T, preferred_element_type=jnp.float32).astype(jnp.bfloat16)
    grad_heads = grad_heads.reshape(replicas, blocks, BLK, local_width)
    offsets = offset_list(HOPS)
    outgoing = [
        jnp.take(paired, send_blocks[0, slot_group], axis=1) for slot_group in range(len(offsets))
    ]
    arrived = [None] * len(offsets)
    for slot_group in range(len(offsets)):
        arrived[slot_group] = shifted(outgoing[slot_group], "dom", offsets[slot_group])
    key_pool = jnp.concatenate([paired] + arrived, axis=1)
    own_blocks = jnp.arange(blocks, dtype=jnp.int32)[:, None]
    key_index = jnp.concatenate([own_blocks, neighbor_blocks], axis=1)
    mixed_rows, query_grad, pool_grad = attend(queries, key_pool, key_index, grad_heads, head_count)
    own_grad = pool_grad[:, :blocks]
    remote = pool_grad[:, blocks:].astype(jnp.bfloat16)
    leaving = [
        remote[:, slot_group * SEND : (slot_group + 1) * SEND] for slot_group in range(len(offsets))
    ]
    returned = [None] * len(offsets)
    for slot_group in range(len(offsets)):
        returned[slot_group] = shifted(leaving[slot_group], "dom", -offsets[slot_group])
    returned_stack = jnp.stack(returned, axis=1).astype(jnp.float32)
    chooser = (
        send_blocks[0][:, :, None] == jnp.arange(blocks, dtype=jnp.int32)[None, None, :]
    ).astype(jnp.float32)
    incoming = jnp.einsum(
        "icj,ricqe->rjqe", chooser, returned_stack, precision=lax.Precision.HIGHEST
    )
    pair_grad = (own_grad + incoming).astype(jnp.bfloat16).reshape(-1, 2 * local_width)
    key_grad = pair_grad[:, :local_width]
    value_grad = pair_grad[:, local_width:]
    flat_query_grad = query_grad.reshape(-1, local_width)
    flat_mixed = mixed_rows.reshape(-1, local_width)
    update_term = jnp.dot(flat_mixed, w_out, preferred_element_type=jnp.float32)
    unit_term = jnp.dot(flat_query_grad, w_query.T, preferred_element_type=jnp.float32)
    unit_term = unit_term + jnp.dot(key_grad, w_key.T, preferred_element_type=jnp.float32)
    unit_term = unit_term + jnp.dot(value_grad, w_value.T, preferred_element_type=jnp.float32)
    slab_width = widths // lax.axis_size("tensor")
    offset_start = lax.axis_index("tensor") * slab_width
    flat_normed = normed.reshape(-1, widths)
    normed_own = lax.dynamic_slice_in_dim(flat_normed, offset_start, slab_width, 1)
    update_sum, unit_sum = (
        lax.psum(update_term.astype(jnp.bfloat16), "tensor").astype(jnp.float32),
        lax.psum(unit_term.astype(jnp.bfloat16), "tensor").astype(jnp.float32),
    )
    row_mean = jnp.mean(unit_sum * flat_normed, axis=-1, keepdims=True)
    update_own = lax.dynamic_slice_in_dim(update_sum, offset_start, slab_width, 1)
    unit_own = lax.dynamic_slice_in_dim(unit_sum, offset_start, slab_width, 1)
    update = update_own.astype(jnp.bfloat16).reshape(replicas, node_count, slab_width)
    branch_grad = (inverse.reshape(-1, 1) * (unit_own - normed_own * row_mean)).astype(jnp.bfloat16)
    branch_grad = branch_grad.reshape(replicas, node_count, slab_width)
    total_rows = replicas * node_count * lax.axis_size("dp") * lax.axis_size("dom")
    factor = 1.0 / math.sqrt(total_rows)
    grad_terms = (
        jnp.dot(flat_unit.T, flat_query_grad, preferred_element_type=jnp.float32),
        jnp.dot(flat_unit.T, key_grad, preferred_element_type=jnp.float32),
        jnp.dot(flat_unit.T, value_grad, preferred_element_type=jnp.float32),
        jnp.dot(flat_mixed.T, flat_cot, preferred_element_type=jnp.float32),
    )
    summed_grads = lax.psum(
        (grad_terms[0], grad_terms[1], grad_terms[2], grad_terms[3]), ("dp", "dom")
    )
    return (
        update,
        branch_grad,
        summed_grads[0] * factor,
        summed_grads[1] * factor,
        summed_grads[2] * factor,
        summed_grads[3] * factor,
    )


def solution(mesh):
    placed = (
        P("dp", "dom", None),
        P(None, "tensor"),
        P(None, "tensor"),
        P(None, "tensor"),
        P("tensor", None),
        P("dom", None, None),
        P("dom", None),
        P("dp", "dom", None),
    )
    return jax.shard_map(
        body,
        mesh=mesh,
        in_specs=placed,
        out_specs=(
            P("dp", "dom", "tensor"),
            P("dp", "dom", "tensor"),
            P(None, "tensor"),
            P(None, "tensor"),
            P(None, "tensor"),
            P("tensor", None),
        ),
        check_vma=False,
    )
```

profile of v0, /device:TPU:0, one launch (start us, length us, event | category | flops | bytes accessed | tf_op | source)
XLA Modules:
  0.0 236.0 jit_solution(13203431752200805455)
XLA Ops:
  8.3 1.2 fusion.25
  9.6 1.5 convolution_convert_fusion.1
  11.7 3.1 %collective-permute-start = (bf16[1,2,128,256]{3,2,1,0:T(8,128)(2,1)S(1)}, bf16[1,2,128,256]{3,2,1,0:T(8,128)(2,1)S(1)}, u32[]{:S(2)}, u32[]{:S(2)}) collective-permute-start(bf16[1,2,128,256]{3,2,1,0:T(8,128)(2,1)S(1)} %bitcast_select_fusion.3), channel_id=1, source_target_pairs={{12,0},{0,4},{4,8},{8,12},{13,1},{1,5},{5,9},{9,13},{14,2},{2,6},{... | collective-permute-start | bytes 393224 | tf_op jit(solution)/shard_map/ppermute | solution.py:17
  15.5 2.1 collective-permute-start.1
  20.7 1.9 collective-permute-start.3
  26.1 5.7 %collective-permute-done.2 = bf16[1,2,128,256]{3,2,1,0:T(8,128)(2,1)S(1)} collective-permute-done((bf16[1,2,128,256]{3,2,1,0:T(8,128)(2,1)S(1)}, bf16[1,2,128,256]{3,2,1,0:T(8,128)(2,1)S(1)}, u32[]{:S(2)}, u32[]{:S(2)}) %collective-permute-start.2) | collective-permute-done | bytes 131104 | tf_op jit(solution)/shard_map/ppermute | solution.py:17
  31.8 2.7 %collective-permute-done.3 = bf16[1,2,128,256]{3,2,1,0:T(8,128)(2,1)} collective-permute-done((bf16[1,2,128,256]{3,2,1,0:T(8,128)(2,1)}, bf16[1,2,128,256]{3,2,1,0:T(8,128)(2,1)}, u32[]{:S(2)}, u32[]{:S(2)}) %collective-permute-start.3) | collective-permute-done | bytes 131104 | tf_op jit(solution)/shard_map/ppermute | solution.py:17
  35.4 1.7 gather_fusion
  37.1 4.0 %reshape.290 = bf16[1,4,512,2,2,64]{5,4,3,2,1,0:T(2,128)(2,1)S(1)} reshape(bf16[16,128,256]{2,1,0:T(8,128)(2,1)} %gather_fusion) | data formatting | bytes 2097152 | tf_op jit(solution)/shard_map/jit(_take)/gather | solution.py:43
  41.1 4.3 %copy.33 = bf16[1,4,512,2,2,64]{2,5,4,1,3,0:T(8,128)(2,1)} copy(bf16[1,4,512,2,2,64]{5,4,3,2,1,0:T(2,128)(2,1)S(1)} %reshape.290) | data formatting | bytes 2097152 | tf_op jit(solution)/shard_map/jit(_take)/gather | solution.py:43
  45.4 1.4 broadcast_select_fusion
  46.8 2.1 fusion.92
  48.9 1.8 fusion.49
  50.8 1.2 fusion.24
  52.4 9.6 %fusion.21 = bf16[1,4,128,2,64]{2,4,3,1,0:T(8,128)(2,1)} fusion(f32[4,2,128,512]{3,2,1,0:T(8,128)} %fusion.49, bf16[1,4,512,2,2,64]{2,5,4,1,3,0:T(8,128)(2,1)S(1)} %broadcast_select_fusion, f32[4,2,128,512]{3,2,1,0:T(8,128)} %get-tuple-element.24, f32[4,2,128]{2,1,0:T(2,128)S(1)} %get-tuple-element.23), kind=kOutput, calls=%fused_computation.33 | convolution fusion | flops 70845952 | bytes 9052160 | tf_op jit(solution)/shard_map/rbhqk,rbkhe->rbqhe/dot_general | solution.py:35
  62.1 9.1 %fusion.12 = f32[1,4,512,1,2,64]{2,5,4,1,3,0:T(8,128)S(1)} fusion(bf16[4,128,2,64]{1,3,2,0:T(8,128)(2,1)S(1)} %copy-done.9, f32[4,2,128,512]{3,2,1,0:T(8,128)} %fusion.49, f32[4,2,128,512]{3,2,1,0:T(8,128)} %get-tuple-element.24, f32[4,2,128]{2,1,0:T(2,128)S(1)} %get-tuple-element.23), kind=kOutput, calls=%fused_computation.17 | convolution fusion | flops 70780416 | bytes 5378048 | tf_op jit(solution)/shard_map/rbhqk,rbqhe->rbkhe/dot_general | solution.py:35
  72.2 1.3 fusion.60
  73.5 1.1 fusion.43
  75.2 1.8 reshape.210
  77.0 2.9 %copy.43 = f32[4,4,128,256]{3,1,0,2:T(4,128)S(1)} copy(f32[4,4,128,256]{2,1,3,0:T(4,128)} %reshape.210) | data formatting | bytes 4194304 | tf_op jit(solution)/shard_map/reshape.43
  79.9 1.6 fusion.93
  82.0 2.9 %collective-permute-start.6 = (bf16[1,2,128,256]{3,1,2,0:T(2,128)(2,1)S(1)}, bf16[1,2,128,256]{3,1,2,0:T(2,128)(2,1)S(1)}, u32[]{:S(2)}, u32[]{:S(2)}) collective-permute-start(bf16[1,2,128,256]{3,1,2,0:T(2,128)(2,1)S(1)} %get-tuple-element.21), channel_id=1, source_target_pairs={{8,0},{12,4},{0,8},{4,12},{9,1},{13,5},{1,9},{5,13},{10,2},{14,6},... | collective-permute-start | bytes 393224 | tf_op jit(solution)/shard_map/ppermute | solution.py:17
  85.0 3.8 %collective-permute-start.4 = (bf16[1,2,128,256]{3,1,2,0:T(2,128)(2,1)S(1)}, bf16[1,2,128,256]{3,1,2,0:T(2,128)(2,1)S(1)}, u32[]{:S(2)}, u32[]{:S(2)}) collective-permute-start(bf16[1,2,128,256]{3,1,2,0:T(2,128)(2,1)S(1)} %get-tuple-element.19), channel_id=1, source_target_pairs={{4,0},{8,4},{12,8},{0,12},{5,1},{9,5},{13,9},{1,13},{6,2},{10,6},{... | collective-permute-start | bytes 393224 | tf_op jit(solution)/shard_map/ppermute | solution.py:17
  89.9 6.0 %collective-permute-done.7 = bf16[1,2,128,256]{3,1,2,0:T(2,128)(2,1)S(1)} collective-permute-done((bf16[1,2,128,256]{3,1,2,0:T(2,128)(2,1)S(1)}, bf16[1,2,128,256]{3,1,2,0:T(2,128)(2,1)S(1)}, u32[]{:S(2)}, u32[]{:S(2)}) %collective-permute-start.7) | collective-permute-done | bytes 131104 | tf_op jit(solution)/shard_map/ppermute | solution.py:17
  95.9 2.8 %collective-permute-done.6 = bf16[1,2,128,256]{3,1,2,0:T(2,128)(2,1)S(1)} collective-permute-done((bf16[1,2,128,256]{3,1,2,0:T(2,128)(2,1)S(1)}, bf16[1,2,128,256]{3,1,2,0:T(2,128)(2,1)S(1)}, u32[]{:S(2)}, u32[]{:S(2)}) %collective-permute-start.6) | collective-permute-done | bytes 131104 | tf_op jit(solution)/shard_map/ppermute | solution.py:17
  105.1 34.4 %all-reduce.7.cloned.1.call-done = (bf16[512,512]{1,0:T(8,128)(2,1)}, bf16[512,512]{1,0:T(8,128)(2,1)}) async-done(((bf16[512,512]{1,0:T(8,128)(2,1)}, bf16[512,512]{1,0:T(8,128)(2,1)}), (bf16[512,512]{1,0:T(8,128)(2,1)}, bf16[512,512]{1,0:T(8,128)(2,1)})) %all-reduce.7.cloned.1.call-update) | async-done | bytes 1048592 | tf_op jit(solution)/shard_map/psum | solution.py:133
  139.5 1.2 convert_element_type.84
  140.8 1.6 fusion.57
  143.6 80.4 %all-reduce.5.cloned.1.call-done = (f32[512,128]{1,0:T(8,128)}, f32[512,128]{1,0:T(8,128)}, f32[512,128]{1,0:T(8,128)}, f32[128,512]{1,0:T(8,128)}) async-done(((f32[512,128]{1,0:T(8,128)}, f32[512,128]{1,0:T(8,128)}, f32[512,128]{1,0:T(8,128)}, f32[128,512]{1,0:T(8,128)}), (f32[512,128]{1,0:T(8,128)}, f32[512,128]{1,0:T(8,128)}, f32[512,128]{1,0:T(8,128)}, ...) | async-done | bytes 1048592 | tf_op jit(solution)/shard_map/psum | solution.py:150
  224.0 1.7 broadcast_multiply_fusion.3
  225.7 1.7 broadcast_multiply_fusion
  227.3 1.9 broadcast_multiply_fusion.1
  (100 shorter events, 21.0 us)
Async XLA Ops:
  7.2 16.1 %copy-start = (bf16[1,512,512]{2,1,0:T(8,128)(2,1)S(1)}, bf16[1,512,512]{2,1,0:T(8,128)(2,1)}, u32[]{:S(2)}) copy-start(bf16[1,512,512]{2,1,0:T(8,128)(2,1)} %param.17) | copy-start | bytes 1572868
  7.2 15.7 %copy-start.1 = (bf16[1,512,512]{2,1,0:T(8,128)(2,1)S(1)}, bf16[1,512,512]{2,1,0:T(8,128)(2,1)}, u32[]{:S(2)}) copy-start(bf16[1,512,512]{2,1,0:T(8,128)(2,1)} %param.10) | copy-start | bytes 1572868
  7.2 15.4 %copy-start.13 = (s32[4,3]{1,0:T(4,128)S(1)}, s32[4,3]{1,0:T(4,128)}, u32[]{:S(2)}) copy-start(s32[4,3]{1,0:T(4,128)} %param.16) | copy-start | bytes 148
  7.2 15.7 %copy-start.6 = (bf16[512,128]{1,0:T(8,128)(2,1)S(1)}, bf16[512,128]{1,0:T(8,128)(2,1)}, u32[]{:S(2)}) copy-start(bf16[512,128]{1,0:T(8,128)(2,1)} %param.11) | copy-start | bytes 393220
  7.2 132.3 %all-reduce.7.cloned.1.call-start = ((), (), s32[]{:S(2)}) async-start(), calls=%async_computation.1 | async-start | bytes 2097152 | tf_op jit(solution)/shard_map/psum | solution.py:133
  9.6 13.7 %copy-start.4 = (bf16[128,512]{1,0:T(8,128)(2,1)S(1)}, bf16[128,512]{1,0:T(8,128)(2,1)}, u32[]{:S(2)}) copy-start(bf16[128,512]{1,0:T(8,128)(2,1)} %param.14) | copy-start | bytes 393220
  11.7 14.3 %collective-permute-start = (bf16[1,2,128,256]{3,2,1,0:T(8,128)(2,1)S(1)}, bf16[1,2,128,256]{3,2,1,0:T(8,128)(2,1)S(1)}, u32[]{:S(2)}, u32[]{:S(2)}) collective-permute-start(bf16[1,2,128,256]{3,2,1,0:T(8,128)(2,1)S(1)} %bitcast_select_fusion.3), channel_id=1, source_target_pairs={{12,0},{0,4},{4,8},{8,12},{13,1},{1,5},{5,9},{9,13},{14,2},{2,6},{... | collective-permute-start | bytes 393224 | tf_op jit(solution)/shard_map/ppermute | solution.py:17
  15.5 10.6 %collective-permute-start.1 = (bf16[1,2,128,256]{3,2,1,0:T(8,128)(2,1)S(1)}, bf16[1,2,128,256]{3,2,1,0:T(8,128)(2,1)S(1)}, u32[]{:S(2)}, u32[]{:S(2)}) collective-permute-start(bf16[1,2,128,256]{3,2,1,0:T(8,128)(2,1)S(1)} %bitcast_select_fusion.2), channel_id=1, source_target_pairs={{4,0},{8,4},{12,8},{0,12},{5,1},{9,5},{13,9},{1,13},{6,2},{10,6},{... | collective-permute-start | bytes 393224 | tf_op jit(solution)/shard_map/ppermute | solution.py:17
  18.3 13.5 %collective-permute-start.2 = (bf16[1,2,128,256]{3,2,1,0:T(8,128)(2,1)S(1)}, bf16[1,2,128,256]{3,2,1,0:T(8,128)(2,1)S(1)}, u32[]{:S(2)}, u32[]{:S(2)}) collective-permute-start(bf16[1,2,128,256]{3,2,1,0:T(8,128)(2,1)S(1)} %bitcast_select_fusion.1), channel_id=1, source_target_pairs={{8,0},{12,4},{0,8},{4,12},{9,1},{13,5},{1,9},{5,13},{10,2},{14,6},... | collective-permute-start | bytes 393224 | tf_op jit(solution)/shard_map/ppermute | solution.py:17
  19.9 5.5 %copy-start.11 = (s32[1,4,2]{1,2,0:T(2,128)S(1)}, s32[1,4,2]{1,2,0:T(2,128)}, u32[]{:S(2)}) copy-start(s32[1,4,2]{1,2,0:T(2,128)} %param.15) | copy-start | bytes 100
  20.7 13.8 %collective-permute-start.3 = (bf16[1,2,128,256]{3,2,1,0:T(8,128)(2,1)}, bf16[1,2,128,256]{3,2,1,0:T(8,128)(2,1)}, u32[]{:S(2)}, u32[]{:S(2)}) collective-permute-start(bf16[1,2,128,256]{3,2,1,0:T(8,128)(2,1)} %bitcast_select_fusion), channel_id=1, source_target_pairs={{8,0},{12,4},{0,8},{4,12},{9,1},{13,5},{1,9},{5,13},{10,2},{14,6},... | collective-permute-start | bytes 393224 | tf_op jit(solution)/shard_map/ppermute | solution.py:17
  45.4 1.4 copy-start.8
  48.9 1.9 copy-start.14
  52.4 9.6 %copy-start.9 = (bf16[4,128,2,64]{1,3,2,0:T(8,128)(2,1)S(1)}, bf16[4,128,2,64]{1,3,2,0:T(8,128)(2,1)}, u32[]{:S(2)}) copy-start(bf16[4,128,2,64]{1,3,2,0:T(8,128)(2,1)} %copy.35) | copy-start | bytes 393220
  71.2 3.5 %copy-start.10 = (bf16[1,4,128,2,64]{2,4,3,1,0:T(8,128)(2,1)S(1)}, bf16[1,4,128,2,64]{2,4,3,1,0:T(8,128)(2,1)}, u32[]{:S(2)}) copy-start(bf16[1,4,128,2,64]{2,4,3,1,0:T(8,128)(2,1)} %fusion.24) | copy-start | bytes 393220
  79.9 18.8 %copy-start.12 = (s32[4,2]{1,0:T(4,128)S(1)}, s32[4,2]{1,0:T(4,128)}, u32[]{:S(2)}) copy-start(s32[4,2]{1,0:T(4,128)} %copy.44) | copy-start | bytes 100
  82.0 13.9 %collective-permute-start.7 = (bf16[1,2,128,256]{3,1,2,0:T(2,128)(2,1)S(1)}, bf16[1,2,128,256]{3,1,2,0:T(2,128)(2,1)S(1)}, u32[]{:S(2)}, u32[]{:S(2)}) collective-permute-start(bf16[1,2,128,256]{3,1,2,0:T(2,128)(2,1)S(1)} %get-tuple-element.20), channel_id=1, source_target_pairs={{8,0},{12,4},{0,8},{4,12},{9,1},{13,5},{1,9},{5,13},{10,2},{14,6},... | collective-permute-start | bytes 393224 | tf_op jit(solution)/shard_map/ppermute | solution.py:17
  82.0 16.7 %collective-permute-start.6 = (bf16[1,2,128,256]{3,1,2,0:T(2,128)(2,1)S(1)}, bf16[1,2,128,256]{3,1,2,0:T(2,128)(2,1)S(1)}, u32[]{:S(2)}, u32[]{:S(2)}) collective-permute-start(bf16[1,2,128,256]{3,1,2,0:T(2,128)(2,1)S(1)} %get-tuple-element.21), channel_id=1, source_target_pairs={{8,0},{12,4},{0,8},{4,12},{9,1},{13,5},{1,9},{5,13},{10,2},{14,6},... | collective-permute-start | bytes 393224 | tf_op jit(solution)/shard_map/ppermute | solution.py:17
  84.9 13.8 %collective-permute-start.5 = (bf16[1,2,128,256]{3,1,2,0:T(2,128)(2,1)S(1)}, bf16[1,2,128,256]{3,1,2,0:T(2,128)(2,1)S(1)}, u32[]{:S(2)}, u32[]{:S(2)}) collective-permute-start(bf16[1,2,128,256]{3,1,2,0:T(2,128)(2,1)S(1)} %get-tuple-element.22), channel_id=1, source_target_pairs={{12,0},{0,4},{4,8},{8,12},{13,1},{1,5},{5,9},{9,13},{14,2},{2,6},{... | collective-permute-start | bytes 393224 | tf_op jit(solution)/shard_map/ppermute | solution.py:17
  85.0 13.8 %collective-permute-start.4 = (bf16[1,2,128,256]{3,1,2,0:T(2,128)(2,1)S(1)}, bf16[1,2,128,256]{3,1,2,0:T(2,128)(2,1)S(1)}, u32[]{:S(2)}, u32[]{:S(2)}) collective-permute-start(bf16[1,2,128,256]{3,1,2,0:T(2,128)(2,1)S(1)} %get-tuple-element.19), channel_id=1, source_target_pairs={{4,0},{8,4},{12,8},{0,12},{5,1},{9,5},{13,9},{1,13},{6,2},{10,6},{... | collective-permute-start | bytes 393224 | tf_op jit(solution)/shard_map/ppermute | solution.py:17
  98.7 1.2 copy-start.2
  98.7 1.2 copy-start.7
  99.6 1.0 copy-start.5
  101.7 122.3 %all-reduce.5.cloned.1.call-start = ((), (), s32[]{:S(2)}) async-start(), calls=%async_computation | async-start | bytes 2097152 | tf_op jit(solution)/shard_map/psum | solution.py:150
  139.5 2.8 %copy-start.3 = (bf16[512,512]{1,0:T(8,128)(2,1)S(1)}, bf16[512,512]{1,0:T(8,128)(2,1)}, u32[]{:S(2)}) copy-start(bf16[512,512]{1,0:T(8,128)(2,1)} %get-tuple-element.16) | copy-start | bytes 1572868
Sparse Core Ops, SparseCore 0:
  101.8 37.6 all-reduce.6
  144.5 79.4 all-reduce.4
where the time goes:
time: 237 us; the launch traced here: 236 us
  waiting for transfers between devices  132 us (56%)
  matrix products  37 us (16%)
  local copies, waits for them, and re-layouts  23.5 us (10%)
  starting transfers between devices  15.1 us (6%)
  between operations  14.5 us (6%)
  other arithmetic  13.9 us (6%)
    psum x1, waiting for transfers between devices, body(): lax.psum((grad_terms[0], grad_terms[1], grad_terms[2], grad_terms[3]), ('...  80.4 us
    psum x1, waiting for transfers between devices, body(): lax.psum(update_term.astype(jnp.bfloat16), 'tensor').astype(jnp.float32)  34.4 us
    dot_general x5, matrix products, product(): return jnp.einsum(form, left, right, preferred_element_type=jnp.float32)  22.1 us
    ppermute x8, waiting for transfers between devices, shifted(): return lax.ppermute(block, axis, route)  17.2 us
    ppermute x8, starting transfers between devices, shifted(): return lax.ppermute(block, axis, route)  15 us
    gather x3, local copies, waits for them, and re-layouts, attend(): chosen = jnp.take(key_pool, key_index.reshape(-1), axis=1)  9.96 us
    another operation x6, local copies, waits for them, and re-layouts  5.89 us
  transfers between devices with their start and end apart: 10, of which 6 were waited for; matrix products, arithmetic and copies ran while one was open for 6% of the time, Pallas kernels for 0%

commit v1 on v0

v1 whole, which is shorter than its diff:
```python
import functools
import math

import jax
import jax.numpy as jnp
from jax import lax
from jax.experimental import pallas as pl
from jax.experimental.pallas import tpu as pltpu
from jax.sharding import PartitionSpec as P

BLK = 128
HOPS = 2
SEND = 2
HD = 64
PAD = 16
EPS = 1e-05
LIMIT = 48 * 1024 * 1024
F32 = jnp.float32
BF16 = jnp.bfloat16


def offset_list(hops):
    result = []
    for section in range(1, hops + 1):
        result.append(section)
        result.append(-section)
    return result


def piece_order(ranks, offsets):
    count = offsets * SEND
    share = count // ranks
    if share == SEND and offsets == 4:
        return [0, 1, 4, 5, 2, 3, 6, 7], share
    return list(range(count)), share


def nt(left, right):
    return lax.dot_general(left, right, (((1,), (1,)), ((), ())), preferred_element_type=F32)


def nn(left, right):
    return jnp.dot(left, right, preferred_element_type=F32)


def unit_of(rows):
    values = rows.astype(F32)
    return (values * lax.rsqrt(jnp.mean(values * values, axis=-1, keepdims=True) + EPS)).astype(BF16)


def block_at(index, size=BLK):
    return pl.ds(pl.multiple_of(index * size, size), size)


def pick_kernel(share, order_ref, place_ref, send_ref, states_ref, out_ref):
    for inner in range(share):
        block = send_ref[order_ref[place_ref[0] * share + inner]]
        out_ref[inner * BLK : (inner + 1) * BLK, :] = states_ref[block_at(block), :]


def pick_blocks(states, order, place, send, share):
    vmem = pl.BlockSpec(memory_space=pltpu.VMEM)
    smem = pl.BlockSpec(memory_space=pltpu.SMEM)
    return pl.pallas_call(
        functools.partial(pick_kernel, share),
        out_shape=jax.ShapeDtypeStruct((share * BLK, states.shape[1]), BF16),
        in_specs=[smem] * 3 + [vmem],
        out_specs=vmem,
        name="pick_blocks",
    )(order, place, send, states)


def layer_kernel(cfg, *refs):
    ranks, share, blocks, offsets, width = cfg
    place_ref, canon_ref, near_ref, states_ref = refs[:4]
    piece_refs = refs[4 : 4 + ranks]
    cot_ref, wq_ref, wk_ref, wv_ref, wo_ref = refs[4 + ranks : 9 + ranks]
    far_keep, far_send, own_keep, own_send, g_keep, g_send = refs[9 + ranks : 15 + ranks]
    unit_ref, k_ref, v_ref, kt_ref, vt_ref, ka_ref, va_ref, mixed_ref, dq_ref = refs[15 + ranks :]
    heads = width // HD
    received = offsets * SEND
    entries = blocks + received
    feats = states_ref.shape[1]
    slabs = feats // width
    sub = BLK // width
    group = SEND * BLK + PAD
    rank = place_ref[0]
    half = place_ref[1]
    odd = (rank & 1) == 1
    upper = rank >> 1

    chunk = 64
    for start in range(0, blocks * BLK, chunk):
        unit_ref[start : start + chunk, :] = unit_of(states_ref[start : start + chunk, :])
    for slot in range(ranks):
        for inner in range(share):
            base = pl.multiple_of((canon_ref[slot * share + inner] + blocks) * BLK, BLK)
            for start in range(0, BLK, chunk):
                source = inner * BLK + start
                unit_ref[pl.ds(pl.multiple_of(base + start, chunk), chunk), :] = unit_of(
                    piece_refs[slot][source : source + chunk, :]
                )

    wkv = jnp.concatenate([wk_ref[...], wv_ref[...]], axis=1)
    queries = nn(unit_ref[: blocks * BLK, :], wq_ref[...])
    grads = nt(cot_ref[...], wo_ref[...])
    for start in range(0, entries, blocks):
        paired = nn(unit_ref[start * BLK : (start + blocks) * BLK, :], wkv)
        for entry in range(blocks):
            rows = paired[entry * BLK : (entry + 1) * BLK]
            keys, values = rows[:, :width], rows[:, width:]
            at = start + entry
            k_ref[at * BLK : (at + 1) * BLK, :] = keys.astype(BF16)
            v_ref[at * BLK : (at + 1) * BLK, :] = values.astype(BF16)
            kt_ref[at] = keys.T.astype(BF16)
            vt_ref[at] = values.T.astype(BF16)
    ka_ref[...] = jnp.zeros_like(ka_ref)
    va_ref[...] = jnp.zeros_like(va_ref)

    lane_head = lax.broadcasted_iota(jnp.int32, (BLK, width), 1) // HD

    def by_head(rows):
        if heads == 1:
            return rows.astype(BF16)
        return jnp.concatenate(
            [jnp.where(lane_head == head, rows, 0.0) for head in range(heads)], axis=0
        ).astype(BF16)

    def diagonal(stacked):
        return jnp.concatenate(
            [
                stacked[head * HD : (head + 1) * HD, head * BLK : (head + 1) * BLK]
                for head in range(heads)
            ],
            axis=0,
        )

    shrink = 1.0 / math.sqrt(HD)
    near = near_ref.shape[1]
    mixed_t, dq_t = [], []
    for block in range(blocks):
        listed = [block] + [near_ref[block, n] for n in range(near)]
        keys = jnp.concatenate([k_ref[block_at(e), :] for e in listed], axis=0)
        values = jnp.concatenate([v_ref[block_at(e), :] for e in listed], axis=0)
        keys_t = jnp.concatenate([kt_ref[e] for e in listed], axis=1)
        values_t = jnp.concatenate([vt_ref[e] for e in listed], axis=1)
        q_all = by_head(queries[block * BLK : (block + 1) * BLK])
        g_all = by_head(grads[block * BLK : (block + 1) * BLK].astype(BF16).astype(F32))
        scores = nt(keys, q_all) * shrink
        powers = jnp.exp(scores - jnp.max(scores, axis=0, keepdims=True))
        weights = powers / jnp.sum(powers, axis=0, keepdims=True)
        low = weights.astype(BF16)
        mix = diagonal(nn(values_t, low))
        mixed_t.append(mix.astype(BF16))
        mixed_ref[block * BLK : (block + 1) * BLK, :] = mix.T.astype(BF16)
        prob = nt(values, g_all)
        drop = jnp.sum(weights * prob, axis=0, keepdims=True)
        score_low = (weights * (prob - drop) * shrink).astype(BF16)
        dq = diagonal(nn(keys_t, score_low))
        dq_t.append(dq.astype(BF16))
        dq_ref[block * BLK : (block + 1) * BLK, :] = dq.T.astype(BF16)
        dk = nn(score_low, q_all)
        dv = nn(low, g_all)
        for n, e in enumerate(listed):
            ka_ref[block_at(e), :] += dk[n * BLK : (n + 1) * BLK]
            va_ref[block_at(e), :] += dv[n * BLK : (n + 1) * BLK]

    ones = jnp.ones((16, feats), BF16)

    def put(keep_ref, send_ref, row, values):
        count = values.shape[0]
        for pair in range(slabs // 2):
            left = values[:, 2 * pair * width : (2 * pair + 1) * width]
            right = values[:, (2 * pair + 1) * width : (2 * pair + 2) * width]
            at = upper ^ pair
            keep_ref[at, row : row + count, :] = jnp.where(odd, right, left).astype(BF16)
            send_ref[at, row : row + count, :] = jnp.where(odd, left, right).astype(BF16)

    def put_dots(keep_ref, send_ref, row, dots):
        parts = []
        for dot in dots:
            for piece in range(sub):
                parts.append(dot[:1, piece * width : (piece + 1) * width])
        parts.append(jnp.zeros((PAD - len(parts), width), F32))
        rows = jnp.concatenate(parts, axis=0).astype(BF16)
        for pair in range(slabs // 2):
            keep_ref[pair, row : row + PAD, :] = rows
            send_ref[pair, row : row + PAD, :] = rows

    def row_dot(term, first):
        product = (term * unit_ref[first : first + BLK, :].astype(F32)).astype(BF16)
        return nt(ones, product)

    wkv_b = wkv
    for offset in range(offsets):
        first = (blocks + offset * SEND) * BLK
        both = jnp.concatenate(
            [ka_ref[first : first + SEND * BLK, :], va_ref[first : first + SEND * BLK, :]], axis=1
        ).astype(BF16)
        term = nt(both, wkv_b)
        put(far_keep, far_send, offset * group, term)
        dots = [
            row_dot(term[c * BLK : (c + 1) * BLK], first + c * BLK) for c in range(SEND)
        ]
        put_dots(far_keep, far_send, offset * group + SEND * BLK, dots)

    own_rows = blocks * BLK
    dots = []
    for pair in range(0, blocks, 2):
        first, last = pair * BLK, (pair + 2) * BLK
        both = jnp.concatenate([ka_ref[first:last, :], va_ref[first:last, :]], axis=1).astype(BF16)
        term = nt(both, wkv_b) + nt(dq_ref[first:last, :], wq_ref[...])
        put(own_keep, own_send, first, term)
        dots += [row_dot(term[c * BLK : (c + 1) * BLK], first + c * BLK) for c in range(2)]
        update = nn(mixed_ref[first:last, :], wo_ref[...])
        put(own_keep, own_send, own_rows + PAD + first, update)
    put_dots(own_keep, own_send, own_rows, dots)

    own_unit = unit_ref[:own_rows, :]
    grad_q = nn(jnp.concatenate(dq_t, axis=1), own_unit)
    grad_out = nn(jnp.concatenate(mixed_t, axis=1), cot_ref[...])

    def turned(ref):
        return jnp.concatenate(
            [ref[e * BLK : (e + 1) * BLK, :].T.astype(BF16) for e in range(entries)], axis=1
        )

    grad_k = nn(turned(ka_ref), unit_ref[...])
    grad_v = nn(turned(va_ref), unit_ref[...])
    second = half == 1
    g_keep[:width, :] = jnp.where(second, grad_v, grad_q).astype(BF16)
    g_keep[width:, :] = jnp.where(second, grad_out, grad_k).astype(BF16)
    g_send[:width, :] = jnp.where(second, grad_q, grad_v).astype(BF16)
    g_send[width:, :] = jnp.where(second, grad_k, grad_out).astype(BF16)


def run_layer(ranks, share, offsets, place, canon, near, states, pieces, cot, weights):
    rows, feats = states.shape
    blocks = rows // BLK
    width = weights[0].shape[1]
    entries = blocks + offsets * SEND
    pairs = feats // width // 2
    far_rows = offsets * (SEND * BLK + PAD)
    own_rows = 2 * rows + PAD
    vmem = pl.BlockSpec(memory_space=pltpu.VMEM)
    smem = pl.BlockSpec(memory_space=pltpu.SMEM)
    cfg = (ranks, share, blocks, offsets, width)
    shape = jax.ShapeDtypeStruct
    return pl.pallas_call(
        functools.partial(layer_kernel, cfg),
        out_shape=(
            shape((pairs, far_rows, width), BF16),
            shape((pairs, far_rows, width), BF16),
            shape((pairs, own_rows, width), BF16),
            shape((pairs, own_rows, width), BF16),
            shape((2 * width, feats), BF16),
            shape((2 * width, feats), BF16),
        ),
        in_specs=[smem] * 3 + [vmem] * (6 + ranks),
        out_specs=[vmem] * 6,
        scratch_shapes=[
            pltpu.VMEM((entries * BLK, feats), BF16),
            pltpu.VMEM((entries * BLK, width), BF16),
            pltpu.VMEM((entries * BLK, width), BF16),
            pltpu.VMEM((entries, width, BLK), BF16),
            pltpu.VMEM((entries, width, BLK), BF16),
            pltpu.VMEM((entries * BLK, width), F32),
            pltpu.VMEM((entries * BLK, width), F32),
            pltpu.VMEM((rows, width), BF16),
            pltpu.VMEM((rows, width), BF16),
        ],
        compiler_params=pltpu.CompilerParams(vmem_limit_bytes=LIMIT),
        name="layer",
    )(place, canon, near, states, *pieces, cot, *weights)


def finish_kernel(cfg, *refs):
    blocks, offsets, width, spread = cfg
    place_ref, send_ref, states_ref, mine_ref, other_ref = refs[:5]
    far_refs = refs[5 : 5 + len(spread)]
    update_ref, branch_ref, unit_ref = refs[5 + len(spread) :]
    own_rows = blocks * BLK
    sub = BLK // width
    group = SEND * BLK + PAD
    rank = place_ref[0]

    def both(first, last):
        return mine_ref[first:last, :].astype(F32) + other_ref[first:last, :].astype(F32)

    update_ref[...] = both(own_rows + PAD, 2 * own_rows + PAD).astype(BF16)
    unit_ref[...] = both(0, own_rows)
    dots = both(own_rows, own_rows + PAD)
    at_row = lax.broadcasted_iota(jnp.int32, (PAD, width), 0)
    for ref, members in zip(far_refs, spread):
        for position, offset in enumerate(members):
            first = position * group
            extra = ref[first + SEND * BLK : first + group, :].astype(F32)
            for c in range(SEND):
                block = send_ref[offset, c]
                rows = ref[first + c * BLK : first + (c + 1) * BLK, :].astype(F32)
                unit_ref[block_at(block), :] += rows
                for piece in range(sub):
                    line = extra[c * sub + piece : c * sub + piece + 1, :]
                    dots = dots + jnp.where(at_row == block * sub + piece, line, 0.0)
    feats = states_ref.shape[1]
    for block in range(blocks):
        rows = slice(block * BLK, (block + 1) * BLK)
        values = states_ref[rows, :].astype(F32)
        inverse = lax.rsqrt(jnp.mean(values * values, axis=-1, keepdims=True) + EPS)
        own = values[:, :width]
        for slab in range(1, feats // width):
            own = jnp.where(rank == slab, values[:, slab * width : (slab + 1) * width], own)
        line = jnp.concatenate(
            [dots[block * sub + piece : block * sub + piece + 1, :] for piece in range(sub)], axis=1
        )
        mean = jnp.broadcast_to(line * (1.0 / feats), (BLK, BLK)).T[:, :width]
        branch_ref[rows, :] = (inverse * (unit_ref[rows, :] - own * inverse * mean)).astype(BF16)


def run_finish(place, send, states, mine, other, far, spread):
    rows, feats = states.shape
    width = mine.shape[1]
    vmem = pl.BlockSpec(memory_space=pltpu.VMEM)
    smem = pl.BlockSpec(memory_space=pltpu.SMEM)
    shape = jax.ShapeDtypeStruct
    cfg = (rows // BLK, send.shape[0], width, spread)
    return pl.pallas_call(
        functools.partial(finish_kernel, cfg),
        out_shape=(shape((rows, width), BF16), shape((rows, width), BF16)),
        in_specs=[smem] * 2 + [vmem] * (3 + len(far)),
        out_specs=[vmem] * 2,
        scratch_shapes=[pltpu.VMEM((rows, width), F32)],
        compiler_params=pltpu.CompilerParams(vmem_limit_bytes=LIMIT),
        name="finish",
    )(place, send, states, mine, other, *far)


def grads_kernel(cfg, place_ref, *refs):
    parts, factor = cfg
    mine_refs = refs[:parts]
    other_refs = refs[parts : 2 * parts]
    q_ref, k_ref, v_ref, o_ref, all_ref = refs[2 * parts :]
    half = place_ref[1]
    dom = place_ref[2]
    size = mine_refs[0].shape[0]
    width = q_ref.shape[1]
    for group, side in ((mine_refs, half), (other_refs, 1 - half)):
        for step in range(parts):
            index = side * parts + ((dom + parts - step) & (parts - 1))
            all_ref[block_at(index, size), :] = group[step][...]
    for position, ref in enumerate((q_ref, k_ref, v_ref)):
        for start in range(0, ref.shape[0], BLK):
            rows = all_ref[position * width : (position + 1) * width, start : start + BLK]
            ref[start : start + BLK, :] = rows.astype(F32).T * factor
    o_ref[...] = all_ref[3 * width :, :].astype(F32) * factor


def run_grads(place, mine, other, factor):
    parts = len(mine)
    size, feats = mine[0].shape
    width = parts * size // 2
    vmem = pl.BlockSpec(memory_space=pltpu.VMEM)
    smem = pl.BlockSpec(memory_space=pltpu.SMEM)
    tall = jax.ShapeDtypeStruct((feats, width), F32)
    return pl.pallas_call(
        functools.partial(grads_kernel, (parts, factor)),
        out_shape=(tall, tall, tall, jax.ShapeDtypeStruct((width, feats), F32)),
        in_specs=[smem] + [vmem] * (2 * parts),
        out_specs=[vmem] * 4,
        scratch_shapes=[pltpu.VMEM((4 * width, feats), BF16)],
        compiler_params=pltpu.CompilerParams(vmem_limit_bytes=LIMIT),
        name="weight_grads",
    )(place, *mine, *other)


def swap(array, axis, bit):
    return lax.ppermute(array, axis, [(i, i ^ bit) for i in range(lax.axis_size(axis))])


def shifted(array, axis, distance):
    size = lax.axis_size(axis)
    return lax.ppermute(array, axis, [(i, (i + distance) % size) for i in range(size)])


def added(left, right):
    return (left.astype(F32) + right.astype(F32)).astype(BF16)


def scatter_rest(summed, bit, ranks):
    while summed.shape[0] > 1:
        keep, send = summed[0::2], summed[1::2]
        got = swap(send, "tensor", bit)
        bit *= 2
        if keep.shape[0] == 1:
            return keep[0], got[0]
        summed = added(keep, got)
    return summed[0], None


def body(states, w_query, w_key, w_value, w_out, send_blocks, neighbor_blocks, cotangent):
    replicas, node_count, feats = states.shape
    width = w_query.shape[1]
    ranks = lax.axis_size("tensor")
    parts = lax.axis_size("dom")
    offsets = offset_list(HOPS)
    order, share = piece_order(ranks, len(offsets))
    rank = lax.axis_index("tensor")
    half = lax.axis_index("dp")
    dom = lax.axis_index("dom")
    explicit = parts == 4 and lax.axis_size("dp") == 2
    place = jnp.stack([rank, half if explicit else jnp.zeros_like(half), dom]).astype(jnp.int32)
    table = [
        [order[(slot ^ r) * share + inner] for slot in range(ranks) for inner in range(share)]
        for r in range(ranks)
    ]
    canon = lax.dynamic_index_in_dim(jnp.asarray(table, jnp.int32), rank, 0, keepdims=False)
    flat_states = states.reshape(-1, feats)
    flat_cot = cotangent.reshape(-1, feats)

    leaving = pick_blocks(
        flat_states,
        jnp.asarray(order, jnp.int32),
        place,
        send_blocks.reshape(-1),
        share,
    )
    route = []
    for p in range(parts):
        for r in range(ranks):
            distance = offsets[order[r * share] // SEND]
            route.append((p * ranks + r, ((p + distance) % parts) * ranks + r))
    pieces = [lax.ppermute(leaving, ("dom", "tensor"), route)]
    bit = 1
    levels = []
    while bit < ranks:
        levels.append(bit)
        bit *= 2
    held = {0: pieces[0]}
    for bit in reversed(levels):
        for slot in list(held):
            held[slot ^ bit] = swap(held[slot], "tensor", bit)
    pieces = [held[slot] for slot in range(ranks)]

    far_keep, far_send, own_keep, own_send, g_keep, g_send = run_layer(
        ranks,
        share,
        len(offsets),
        place,
        canon,
        neighbor_blocks,
        flat_states,
        pieces,
        flat_cot,
        (w_query, w_key, w_value, w_out),
    )

    far_got = swap(far_send, "tensor", 1)
    g_got = swap(g_send, "dp", 1) if explicit else None
    own_got = swap(own_send, "tensor", 1)
    far_mine, far_other = scatter_rest(added(far_keep, far_got), 2, ranks)
    far_sum = far_mine if far_other is None else added(far_mine, far_other)
    own_mine, own_other = scatter_rest(added(own_keep, own_got), 2, ranks)
    if own_other is None:
        own_other = jnp.zeros_like(own_mine)

    group = SEND * BLK + PAD
    spread = []
    for index, distance in enumerate(offsets):
        for members in spread:
            if (offsets[members[0]] - distance) % parts == 0 and members[-1] == index - 1:
                members.append(index)
                break
        else:
            spread.append([index])
    far = [
        shifted(
            far_sum[members[0] * group : (members[-1] + 1) * group], "dom", -offsets[members[0]]
        )
        for members in spread
    ]
    spread = tuple(tuple(members) for members in spread)

    total_rows = replicas * node_count * lax.axis_size("dp") * parts
    factor = 1.0 / math.sqrt(total_rows)
    if explicit:
        quarters = added(g_keep, g_got).reshape(parts, -1, feats)
        mine = lax.dynamic_index_in_dim(quarters, dom, 0, keepdims=False).astype(F32)
        for step in range(1, parts):
            leaving = lax.dynamic_index_in_dim(quarters, (dom + step) % parts, 0, keepdims=False)
            mine = mine + shifted(leaving, "dom", step).astype(F32)
        mine = mine.astype(BF16)
        chunks = [mine] + [shifted(mine, "dom", step) for step in range(1, parts)]
        others = [swap(chunk, "dp", 1) for chunk in chunks]
        grads = run_grads(place, chunks, others, factor)
    else:
        summed = lax.psum(
            jnp.concatenate([g_keep, g_send]).astype(F32), ("dp", "dom")
        ).reshape(4, width, feats)
        grads = (
            summed[0].T * factor,
            summed[1].T * factor,
            summed[2].T * factor,
            summed[3] * factor,
        )
    update, branch = run_finish(
        place, send_blocks[0], flat_states, own_mine, own_other, far, spread
    )
    shape = (replicas, node_count, width)
    return (update.reshape(shape), branch.reshape(shape), *grads)


def solution(mesh):
    placed = (
        P("dp", "dom", None),
        P(None, "tensor"),
        P(None, "tensor"),
        P(None, "tensor"),
        P("tensor", None),
        P("dom", None, None),
        P("dom", None),
        P("dp", "dom", None),
    )
    return jax.shard_map(
        body,
        mesh=mesh,
        in_specs=placed,
        out_specs=(
            P("dp", "dom", "tensor"),
            P("dp", "dom", "tensor"),
            P(None, "tensor"),
            P(None, "tensor"),
            P(None, "tensor"),
            P("tensor", None),
        ),
        check_vma=False,
    )
```

time: 237 us -> 91.6 us (0.39)
  waiting for transfers between devices: 132 us -> 41.2 us
  matrix products: 37 us -> 0 us
  local copies, waits for them, and re-layouts: 23.5 us -> 6.8 us
  Pallas kernels: 0 us -> 14 us
  between operations: 14.5 us -> 0.86 us
  other arithmetic: 13.9 us -> 2.1 us
  starting transfers between devices: 15.1 us -> 26.3 us
    psum x2 -> x0, waiting for transfers between devices: 115 us -> none  [the longest x1 80.4 us: body(): lax.psum((grad_terms[0], grad_terms[1], grad_terms[2], grad_terms[3]), ('...]
    dot_general x18 -> x0, matrix products: 34.9 us -> none  [the longest x5 22.1 us: product(): return jnp.einsum(form, left, right, preferred_element_type=jnp.float32)]
    ppermute x8 -> x22, waiting for transfers between devices: 17.2 us -> 41.2 us  [the longest x12 24.4 us: swap(): lax.ppermute(array, axis, [(i, i ^ bit) for i in range(lax.axis_size(axis...]
    pallas_call x0 -> x4, Pallas kernels: none -> 14 us  [the longest x1 8.96 us: run_layer(): pl.pallas_call(functools.partial(layer_kernel, cfg), out_shape=(shape((pa...]
    gather x7 -> x0, local copies, waits for them, and re-layouts: 12.2 us -> none  [the longest x3 9.96 us: attend(): chosen = jnp.take(key_pool, key_index.reshape(-1), axis=1)]
    ppermute x8 -> x22, starting transfers between devices: 15 us -> 26.3 us  [the longest x9 11.8 us: shifted(): lax.ppermute(array, axis, [(i, (i + distance) % size) for i in range(size)])]
    another operation x7 -> x0, local copies, waits for them, and re-layouts: 6.1 us -> none
    mul x4 -> x0, other arithmetic: 5.33 us -> none  [the longest x1 1.85 us: body(): summed_grads[2] * factor]
  transfers between devices with their start and end apart: 10 -> 22, of which waited for: 6 -> 10; matrix products, arithmetic and copies ran while one was open for 6% -> 3% of each run, Pallas kernels for 0% -> 2%
where the time goes in v1:
time: 91.6 us; the launch traced here: 91.3 us
  waiting for transfers between devices  41.2 us (45%)
  starting transfers between devices  26.3 us (29%)
  Pallas kernels  14 us (15%)
  local copies, waits for them, and re-layouts  6.8 us (7%)
  other arithmetic  2.1 us (2%)
    ppermute x12, waiting for transfers between devices, swap(): lax.ppermute(array, axis, [(i, i ^ bit) for i in range(lax.axis_size(axis...  24.4 us
    ppermute x9, starting transfers between devices, shifted(): lax.ppermute(array, axis, [(i, (i + distance) % size) for i in range(size)])  11.8 us
    ppermute x12, starting transfers between devices, swap(): lax.ppermute(array, axis, [(i, i ^ bit) for i in range(lax.axis_size(axis...  11.4 us
    pallas_call x1, Pallas kernels, run_layer(): pl.pallas_call(functools.partial(layer_kernel, cfg), out_shape=(shape((pa...  8.96 us
    ppermute x1, waiting for transfers between devices, body(): pieces = [lax.ppermute(leaving, ('dom', 'tensor'), route)]  8.69 us
    ppermute x9, waiting for transfers between devices, shifted(): lax.ppermute(array, axis, [(i, (i + distance) % size) for i in range(size)])  8.16 us
    unnamed x25, local copies, waits for them, and re-layouts  5.32 us
    ppermute x1, starting transfers between devices, body(): pieces = [lax.ppermute(leaving, ('dom', 'tensor'), route)]  3.02 us
  transfers between devices with their start and end apart: 22, of which 10 were waited for; matrix products, arithmetic and copies ran while one was open for 3% of the time, Pallas kernels for 2%

profile of v1, /device:TPU:0, one launch (start us, length us, event | category | flops | bytes accessed | tf_op | source)
XLA Modules:
  0.0 91.3 jit_solution(7424289093450537945)
XLA Ops:
  0.7 0.8 copy.18
  2.7 1.8 %pick_blocks.1 = bf16[256,512]{1,0:T(8,128)(2,1)} custom-call(s32[8]{0:T(128)} %constant.58.clone.order_ref, s32[3]{0:T(128)} %pad_add_fusion.place_ref.refs_0_, s32[8]{0:T(128)} %reshape.40.send_ref, bf16[512,512]{1,0:T(8,128)(2,1)} %bitcast.29), custom_call_target="tpu_custom_call" | custom-call | tf_op jit(solution)/shard_map/pick_blocks/pallas_call | solution.py:64
  4.5 3.0 %collective-permute-start = (bf16[256,512]{1,0:T(8,128)(2,1)}, bf16[256,512]{1,0:T(8,128)(2,1)S(1)}, u32[]{:S(2)}, u32[]{:S(2)}) collective-permute-start(bf16[256,512]{1,0:T(8,128)(2,1)} %pick_blocks.1), channel_id=1, source_target_pairs={{0,4},{1,9},{2,14},{3,11},{4,8},{5,13},{6,2},{7,15},{8,12},{9,1},{... | collective-permute-start | bytes 786440 | tf_op jit(solution)/shard_map/ppermute | solution.py:432
  7.5 8.7 %collective-permute-done.refs_4_ = bf16[256,512]{1,0:T(8,128)(2,1)S(1)} collective-permute-done((bf16[256,512]{1,0:T(8,128)(2,1)}, bf16[256,512]{1,0:T(8,128)(2,1)S(1)}, u32[]{:S(2)}, u32[]{:S(2)}) %collective-permute-start) | collective-permute-done | bytes 262176 | tf_op jit(solution)/shard_map/ppermute | solution.py:432
  16.2 1.6 %collective-permute-start.1 = (bf16[256,512]{1,0:T(8,128)(2,1)S(1)}, bf16[256,512]{1,0:T(8,128)(2,1)S(1)}, u32[]{:S(2)}, u32[]{:S(2)}) collective-permute-start(bf16[256,512]{1,0:T(8,128)(2,1)S(1)} %collective-permute-done.refs_4_), channel_id=1, source_target_pairs={{0,1},{1,0},{2,3},{3,2},{4,5},{5,4},{6,7},{7,6},{8,9},{9,8},{10,11... | collective-permute-start | bytes 786440 | tf_op jit(solution)/shard_map/ppermute | solution.py:377
  17.8 7.2 %collective-permute-done.2.refs_6_ = bf16[256,512]{1,0:T(8,128)(2,1)S(1)} collective-permute-done((bf16[256,512]{1,0:T(8,128)(2,1)S(1)}, bf16[256,512]{1,0:T(8,128)(2,1)S(1)}, u32[]{:S(2)}, u32[]{:S(2)}) %collective-permute-start.2) | collective-permute-done | bytes 262176 | tf_op jit(solution)/shard_map/ppermute | solution.py:377
  26.5 1.0 %copy-done.1 = bf16[1,512,512]{2,1,0:T(8,128)(2,1)S(1)} copy-done((bf16[1,512,512]{2,1,0:T(8,128)(2,1)S(1)}, bf16[1,512,512]{2,1,0:T(8,128)(2,1)}, u32[]{:S(2)}) %copy-start.1) | copy-done | bytes 524312
  27.6 0.9 copy-done.4
  28.5 0.9 copy-done.5
  29.4 9.0 %layer.1 = (bf16[2,1088,128]{2,1,0:T(8,128)(2,1)S(1)}, bf16[2,1088,128]{2,1,0:T(8,128)(2,1)S(1)}, bf16[2,1040,128]{2,1,0:T(8,128)(2,1)S(1)}, bf16[2,1040,128]{2,...) custom-call(s32[3]{0:T(128)S(1)} %copy-done.6, s32[8]{0:T(128)S(1)} %fusion.3.refs_1_, ...), custom_call_target="tpu_custom_call" | custom-call | tf_op jit(solution)/shard_map/layer/pallas_call | solution.py:249
  38.4 0.8 copy-done.8
  39.2 0.8 copy-done.10
  40.0 1.5 %collective-permute-start.11 = (bf16[256,512]{1,0:T(8,128)(2,1)S(1)}, bf16[256,512]{1,0:T(8,128)(2,1)S(1)}, u32[]{:S(2)}, u32[]{:S(2)}) collective-permute-start(bf16[256,512]{1,0:T(8,128)(2,1)S(1)} %get-tuple-element.25), channel_id=1, source_target_pairs={{0,16},{16,0},{1,17},{17,1},{2,18},{18,2},{3,19},{19,3},{4,20},{20... | collective-permute-start | bytes 786440 | tf_op jit(solution)/shard_map/ppermute | solution.py:377
  41.5 7.0 %collective-permute-done.11 = bf16[256,512]{1,0:T(8,128)(2,1)S(1)} collective-permute-done((bf16[256,512]{1,0:T(8,128)(2,1)S(1)}, bf16[256,512]{1,0:T(8,128)(2,1)S(1)}, u32[]{:S(2)}, u32[]{:S(2)}) %collective-permute-start.11) | collective-permute-done | bytes 262176 | tf_op jit(solution)/shard_map/ppermute | solution.py:377
  48.5 2.0 %collective-permute-start.14 = (bf16[64,512]{1,0:T(8,128)(2,1)S(1)}, bf16[64,512]{1,0:T(8,128)(2,1)S(1)}, u32[]{:S(2)}, u32[]{:S(2)}) collective-permute-start(bf16[64,512]{1,0:T(8,128)(2,1)S(1)} %get-tuple-element.35), channel_id=1, source_target_pairs={{0,12},{4,0},{8,4},{12,8},{1,13},{5,1},{9,5},{13,9},{2,14},{6,2},{... | collective-permute-start | bytes 196616 | tf_op jit(solution)/shard_map/ppermute | solution.py:382
  50.5 1.4 %collective-permute-start.13 = (bf16[64,512]{1,0:T(8,128)(2,1)S(1)}, bf16[64,512]{1,0:T(8,128)(2,1)S(1)}, u32[]{:S(2)}, u32[]{:S(2)}) collective-permute-start(bf16[64,512]{1,0:T(8,128)(2,1)S(1)} %get-tuple-element.36), channel_id=1, source_target_pairs={{0,8},{4,12},{8,0},{12,4},{1,9},{5,13},{9,1},{13,5},{2,10},{6,14},... | collective-permute-start | bytes 196616 | tf_op jit(solution)/shard_map/ppermute | solution.py:382
  53.0 4.0 %collective-permute-done.13 = bf16[64,512]{1,0:T(8,128)(2,1)S(1)} collective-permute-done((bf16[64,512]{1,0:T(8,128)(2,1)S(1)}, bf16[64,512]{1,0:T(8,128)(2,1)S(1)}, u32[]{:S(2)}, u32[]{:S(2)}) %collective-permute-start.13) | collective-permute-done | bytes 65568 | tf_op jit(solution)/shard_map/ppermute | solution.py:382
  57.0 1.0 %collective-permute-done.12 = bf16[64,512]{1,0:T(8,128)(2,1)S(1)} collective-permute-done((bf16[64,512]{1,0:T(8,128)(2,1)S(1)}, bf16[64,512]{1,0:T(8,128)(2,1)S(1)}, u32[]{:S(2)}, u32[]{:S(2)}) %collective-permute-start.12) | collective-permute-done | bytes 65568 | tf_op jit(solution)/shard_map/ppermute | solution.py:382
  58.1 1.4 %collective-permute-start.16 = (bf16[64,512]{1,0:T(8,128)(2,1)S(1)}, bf16[64,512]{1,0:T(8,128)(2,1)S(1)}, u32[]{:S(2)}, u32[]{:S(2)}) collective-permute-start(bf16[64,512]{1,0:T(8,128)(2,1)S(1)} %fusion.2.refs_0_), channel_id=1, source_target_pairs={{0,8},{4,12},{8,0},{12,4},{1,9},{5,13},{9,1},{13,5},{2,10},{6,14},... | collective-permute-start | bytes 196616 | tf_op jit(solution)/shard_map/ppermute | solution.py:382
  59.5 2.6 %collective-permute-start.17 = (bf16[64,512]{1,0:T(8,128)(2,1)S(1)}, bf16[64,512]{1,0:T(8,128)(2,1)S(1)}, u32[]{:S(2)}, u32[]{:S(2)}) collective-permute-start(bf16[64,512]{1,0:T(8,128)(2,1)S(1)} %fusion.2.refs_0_), channel_id=1, source_target_pairs={{0,12},{4,0},{8,4},{12,8},{1,13},{5,1},{9,5},{13,9},{2,14},{6,2},{... | collective-permute-start | bytes 196616 | tf_op jit(solution)/shard_map/ppermute | solution.py:382
  62.1 2.6 %collective-permute-done.15.refs_1_ = bf16[64,512]{1,0:T(8,128)(2,1)S(1)} collective-permute-done((bf16[64,512]{1,0:T(8,128)(2,1)S(1)}, bf16[64,512]{1,0:T(8,128)(2,1)S(1)}, u32[]{:S(2)}, u32[]{:S(2)}) %collective-permute-start.15) | collective-permute-done | bytes 65568 | tf_op jit(solution)/shard_map/ppermute | solution.py:382
  64.7 1.5 %collective-permute-start.18 = (bf16[64,512]{1,0:T(8,128)(2,1)S(1)}, bf16[64,512]{1,0:T(8,128)(2,1)S(1)}, u32[]{:S(2)}, u32[]{:S(2)}) collective-permute-start(bf16[64,512]{1,0:T(8,128)(2,1)S(1)} %fusion.2.refs_0_), channel_id=1, source_target_pairs={{0,16},{16,0},{1,17},{17,1},{2,18},{18,2},{3,19},{19,3},{4,20},{20... | collective-permute-start | bytes 196616 | tf_op jit(solution)/shard_map/ppermute | solution.py:377
  66.7 1.5 %collective-permute-start.20 = (bf16[64,512]{1,0:T(8,128)(2,1)S(1)}, bf16[64,512]{1,0:T(8,128)(2,1)S(1)}, u32[]{:S(2)}, u32[]{:S(2)}) collective-permute-start(bf16[64,512]{1,0:T(8,128)(2,1)S(1)} %collective-permute-done.16.refs_2_), channel_id=1, source_target_pairs={{0,16},{16,0},{1,17},{17,1},{2,18},{18,2},{3,19},{19,3},{4,20},{20... | collective-permute-start | bytes 196616 | tf_op jit(solution)/shard_map/ppermute | solution.py:377
  68.2 1.2 %add_convert_fusion.1 = bf16[2,1040,128]{2,1,0:T(8,128)(2,1)S(1)} fusion(bf16[2,1040,128]{2,1,0:T(8,128)(2,1)} %collective-permute-done.4, bf16[2,1040,128]{2,1,0:T(8,128)(2,1)S(1)} %get-tuple-element.18), kind=kLoop, calls=%fused_computation.1 | loop fusion | flops 1064960 | bytes 1597440 | tf_op jit(solution)/shard_map/convert_element_type | solution.py:386
  69.6 1.7 %collective-permute-start.7 = (bf16[1,1088,128]{2,1,0:T(8,128)(2,1)S(1)}, bf16[1,1088,128]{2,1,0:T(8,128)(2,1)S(1)}, u32[]{:S(2)}, u32[]{:S(2)}) collective-permute-start(bf16[1,1088,128]{2,1,0:T(8,128)(2,1)S(1)} %slice.47), channel_id=1, source_target_pairs={{0,2},{1,3},{2,0},{3,1},{4,6},{5,7},{6,4},{7,5},{8,10},{9,11},{10,... | collective-permute-start | bytes 835592 | tf_op jit(solution)/shard_map/ppermute | solution.py:377
  71.3 6.6 %collective-permute-done.7 = bf16[1,1088,128]{2,1,0:T(8,128)(2,1)S(1)} collective-permute-done((bf16[1,1088,128]{2,1,0:T(8,128)(2,1)S(1)}, bf16[1,1088,128]{2,1,0:T(8,128)(2,1)S(1)}, u32[]{:S(2)}, u32[]{:S(2)}) %collective-permute-start.7) | collective-permute-done | bytes 278560 | tf_op jit(solution)/shard_map/ppermute | solution.py:377
  77.9 1.7 %collective-permute-start.5 = (bf16[1,1040,128]{2,1,0:T(8,128)(2,1)S(1)}, bf16[1,1040,128]{2,1,0:T(8,128)(2,1)S(1)}, u32[]{:S(2)}, u32[]{:S(2)}) collective-permute-start(bf16[1,1040,128]{2,1,0:T(8,128)(2,1)S(1)} %get-tuple-element.30), channel_id=1, source_target_pairs={{0,2},{1,3},{2,0},{3,1},{4,6},{5,7},{6,4},{7,5},{8,10},{9,11},{10,... | collective-permute-start | bytes 798728 | tf_op jit(solution)/shard_map/ppermute | solution.py:377
  79.9 3.2 %collective-permute-start.8 = (bf16[272,128]{1,0:T(8,128)(2,1)S(1)}, bf16[272,128]{1,0:T(8,128)(2,1)S(1)}, u32[]{:S(2)}, u32[]{:S(2)}) collective-permute-start(bf16[272,128]{1,0:T(8,128)(2,1)S(1)} %get-tuple-element.33), channel_id=1, source_target_pairs={{0,12},{4,0},{8,4},{12,8},{1,13},{5,1},{9,5},{13,9},{2,14},{6,2},{... | collective-permute-start | bytes 208904 | tf_op jit(solution)/shard_map/ppermute | solution.py:382
  83.7 1.2 %collective-permute-start.21 = (bf16[64,512]{1,0:T(8,128)(2,1)S(1)}, bf16[64,512]{1,0:T(8,128)(2,1)S(1)}, u32[]{:S(2)}, u32[]{:S(2)}) collective-permute-start(bf16[64,512]{1,0:T(8,128)(2,1)S(1)} %collective-permute-done.17.refs_3_), channel_id=1, source_target_pairs={{0,16},{16,0},{1,17},{17,1},{2,18},{18,2},{3,19},{19,3},{4,20},{20... | collective-permute-start | bytes 196616 | tf_op jit(solution)/shard_map/ppermute | solution.py:377
  85.0 3.0 %collective-permute-done.21.refs_7_ = bf16[64,512]{1,0:T(8,128)(2,1)S(1)} collective-permute-done((bf16[64,512]{1,0:T(8,128)(2,1)S(1)}, bf16[64,512]{1,0:T(8,128)(2,1)S(1)}, u32[]{:S(2)}, u32[]{:S(2)}) %collective-permute-start.21) | collective-permute-done | bytes 65568 | tf_op jit(solution)/shard_map/ppermute | solution.py:377
  88.0 1.6 %weight_grads.1 = (f32[512,128]{1,0:T(8,128)}, f32[512,128]{1,0:T(8,128)}, f32[512,128]{1,0:T(8,128)}, f32[128,512]{1,0:T(8,128)}) custom-call(s32[3]{0:T(128)S(1)} %copy-done.6, bf16[64,512]{1,0:T(8,128)(2,1)S(1)} %fusion.2.refs_0_, bf16[64,512]{1,0:T(8,128)(2,1)S(1)} %collective-permute-done.15.refs_1_, ...), custom_call_target="tpu_custom_call" | custom-call | tf_op jit(solution)/shard_map/weight_grads/pallas_call | solution.py:365
  89.7 1.6 %finish.1 = (bf16[512,128]{1,0:T(8,128)(2,1)}, bf16[512,128]{1,0:T(8,128)(2,1)}) custom-call(s32[3]{0:T(128)S(1)} %copy-done.6, s32[4,2]{1,0:T(4,128)S(1)} %copy.19.refs_1_, bf16[512,512]{1,0:T(8,128)(2,1)S(1)} %bitcast.31, bf16[1040,128]{1,0:T(8,128)(2,1)S(1)} %get-tuple-element.31.refs_3_, bf16[1040,128]{1,0:T(8,128)(2,1)S(1)} %bitcast.33, ...), custom_call_target="tpu_custom_call" | custom-call | tf_op jit(solution)/shard_map/finish/pallas_call | solution.py:327
  (55 shorter events, 5.6 us)
Async XLA Ops:
  0.6 25.9 %copy-start = (bf16[1,512,512]{2,1,0:T(8,128)(2,1)S(1)}, bf16[1,512,512]{2,1,0:T(8,128)(2,1)}, u32[]{:S(2)}) copy-start(bf16[1,512,512]{2,1,0:T(8,128)(2,1)} %param.10) | copy-start | bytes 1572868
  0.6 25.9 %copy-start.7 = (s32[4,3]{1,0:T(4,128)S(1)}, s32[4,3]{1,0:T(4,128)}, u32[]{:S(2)}) copy-start(s32[4,3]{1,0:T(4,128)} %refs_2_.1) | copy-start | bytes 148
  0.7 25.9 %copy-start.2 = (bf16[512,128]{1,0:T(8,128)(2,1)S(1)}, bf16[512,128]{1,0:T(8,128)(2,1)}, u32[]{:S(2)}) copy-start(bf16[512,128]{1,0:T(8,128)(2,1)} %refs_9_.1) | copy-start | bytes 393220
  0.7 25.9 %copy-start.3 = (bf16[512,128]{1,0:T(8,128)(2,1)S(1)}, bf16[512,128]{1,0:T(8,128)(2,1)}, u32[]{:S(2)}) copy-start(bf16[512,128]{1,0:T(8,128)(2,1)} %refs_10_.1) | copy-start | bytes 393220
  2.7 23.8 %copy-start.6 = (s32[3]{0:T(128)S(1)}, s32[3]{0:T(128)}, u32[]{:S(2)}) copy-start(s32[3]{0:T(128)} %pad_add_fusion.place_ref.refs_0_) | copy-start | bytes 40
  4.5 11.7 %collective-permute-start = (bf16[256,512]{1,0:T(8,128)(2,1)}, bf16[256,512]{1,0:T(8,128)(2,1)S(1)}, u32[]{:S(2)}, u32[]{:S(2)}) collective-permute-start(bf16[256,512]{1,0:T(8,128)(2,1)} %pick_blocks.1), channel_id=1, source_target_pairs={{0,4},{1,9},{2,14},{3,11},{4,8},{5,13},{6,2},{7,15},{8,12},{9,1},{... | collective-permute-start | bytes 786440 | tf_op jit(solution)/shard_map/ppermute | solution.py:432
  16.2 8.8 %collective-permute-start.2 = (bf16[256,512]{1,0:T(8,128)(2,1)S(1)}, bf16[256,512]{1,0:T(8,128)(2,1)S(1)}, u32[]{:S(2)}, u32[]{:S(2)}) collective-permute-start(bf16[256,512]{1,0:T(8,128)(2,1)S(1)} %collective-permute-done.refs_4_), channel_id=1, source_target_pairs={{0,2},{1,3},{2,0},{3,1},{4,6},{5,7},{6,4},{7,5},{8,10},{9,11},{10,... | collective-permute-start | bytes 786440 | tf_op jit(solution)/shard_map/ppermute | solution.py:377
  16.2 9.7 %collective-permute-start.1 = (bf16[256,512]{1,0:T(8,128)(2,1)S(1)}, bf16[256,512]{1,0:T(8,128)(2,1)S(1)}, u32[]{:S(2)}, u32[]{:S(2)}) collective-permute-start(bf16[256,512]{1,0:T(8,128)(2,1)S(1)} %collective-permute-done.refs_4_), channel_id=1, source_target_pairs={{0,1},{1,0},{2,3},{3,2},{4,5},{5,4},{6,7},{7,6},{8,9},{9,8},{10,11... | collective-permute-start | bytes 786440 | tf_op jit(solution)/shard_map/ppermute | solution.py:377
  25.0 1.5 %collective-permute-start.3 = (bf16[256,512]{1,0:T(8,128)(2,1)S(1)}, bf16[256,512]{1,0:T(8,128)(2,1)S(1)}, u32[]{:S(2)}, u32[]{:S(2)}) collective-permute-start(bf16[256,512]{1,0:T(8,128)(2,1)S(1)} %collective-permute-done.2.refs_6_), channel_id=1, source_target_pairs={{0,1},{1,0},{2,3},{3,2},{4,5},{5,4},{6,7},{7,6},{8,9},{9,8},{10,11... | collective-permute-start | bytes 786440 | tf_op jit(solution)/shard_map/ppermute | solution.py:377
  26.5 1.0 %copy-start.1 = (bf16[1,512,512]{2,1,0:T(8,128)(2,1)S(1)}, bf16[1,512,512]{2,1,0:T(8,128)(2,1)}, u32[]{:S(2)}) copy-start(bf16[1,512,512]{2,1,0:T(8,128)(2,1)} %param.17) | copy-start | bytes 1572868
  27.6 0.9 copy-start.4
  28.5 0.9 copy-start.5
  40.0 8.5 %collective-permute-start.11 = (bf16[256,512]{1,0:T(8,128)(2,1)S(1)}, bf16[256,512]{1,0:T(8,128)(2,1)S(1)}, u32[]{:S(2)}, u32[]{:S(2)}) collective-permute-start(bf16[256,512]{1,0:T(8,128)(2,1)S(1)} %get-tuple-element.25), channel_id=1, source_target_pairs={{0,16},{16,0},{1,17},{17,1},{2,18},{18,2},{3,19},{19,3},{4,20},{20... | collective-permute-start | bytes 786440 | tf_op jit(solution)/shard_map/ppermute | solution.py:377
  41.4 25.3 %collective-permute-start.4 = (bf16[2,1040,128]{2,1,0:T(8,128)(2,1)}, bf16[2,1040,128]{2,1,0:T(8,128)(2,1)}, u32[]{:S(2)}, u32[]{:S(2)}) collective-permute-start(bf16[2,1040,128]{2,1,0:T(8,128)(2,1)} %copy-done.10), channel_id=1, source_target_pairs={{0,1},{1,0},{2,3},{3,2},{4,5},{5,4},{6,7},{7,6},{8,9},{9,8},{10,11... | collective-permute-start | bytes 1597448 | tf_op jit(solution)/shard_map/ppermute | solution.py:377
  48.5 11.0 %copy-start.9 = (bf16[2,1088,128]{2,1,0:T(8,128)(2,1)S(1)}, bf16[2,1088,128]{2,1,0:T(8,128)(2,1)}, u32[]{:S(2)}) copy-start(bf16[2,1088,128]{2,1,0:T(8,128)(2,1)} %copy-done.8) | copy-start | bytes 1671172
  48.5 4.4 %collective-permute-start.14 = (bf16[64,512]{1,0:T(8,128)(2,1)S(1)}, bf16[64,512]{1,0:T(8,128)(2,1)S(1)}, u32[]{:S(2)}, u32[]{:S(2)}) collective-permute-start(bf16[64,512]{1,0:T(8,128)(2,1)S(1)} %get-tuple-element.35), channel_id=1, source_target_pairs={{0,12},{4,0},{8,4},{12,8},{1,13},{5,1},{9,5},{13,9},{2,14},{6,2},{... | collective-permute-start | bytes 196616 | tf_op jit(solution)/shard_map/ppermute | solution.py:382
  50.5 6.4 %collective-permute-start.13 = (bf16[64,512]{1,0:T(8,128)(2,1)S(1)}, bf16[64,512]{1,0:T(8,128)(2,1)S(1)}, u32[]{:S(2)}, u32[]{:S(2)}) collective-permute-start(bf16[64,512]{1,0:T(8,128)(2,1)S(1)} %get-tuple-element.36), channel_id=1, source_target_pairs={{0,8},{4,12},{8,0},{12,4},{1,9},{5,13},{9,1},{13,5},{2,10},{6,14},... | collective-permute-start | bytes 196616 | tf_op jit(solution)/shard_map/ppermute | solution.py:382
  51.9 6.1 %collective-permute-start.12 = (bf16[64,512]{1,0:T(8,128)(2,1)S(1)}, bf16[64,512]{1,0:T(8,128)(2,1)S(1)}, u32[]{:S(2)}, u32[]{:S(2)}) collective-permute-start(bf16[64,512]{1,0:T(8,128)(2,1)S(1)} %get-tuple-element.34), channel_id=1, source_target_pairs={{0,4},{4,8},{8,12},{12,0},{1,5},{5,9},{9,13},{13,1},{2,6},{6,10},{... | collective-permute-start | bytes 196616 | tf_op jit(solution)/shard_map/ppermute | solution.py:382
  58.0 6.6 %collective-permute-start.15 = (bf16[64,512]{1,0:T(8,128)(2,1)S(1)}, bf16[64,512]{1,0:T(8,128)(2,1)S(1)}, u32[]{:S(2)}, u32[]{:S(2)}) collective-permute-start(bf16[64,512]{1,0:T(8,128)(2,1)S(1)} %fusion.2.refs_0_), channel_id=1, source_target_pairs={{0,4},{4,8},{8,12},{12,0},{1,5},{5,9},{9,13},{13,1},{2,6},{6,10},{... | collective-permute-start | bytes 196616 | tf_op jit(solution)/shard_map/ppermute | solution.py:382
  58.1 8.1 %collective-permute-start.16 = (bf16[64,512]{1,0:T(8,128)(2,1)S(1)}, bf16[64,512]{1,0:T(8,128)(2,1)S(1)}, u32[]{:S(2)}, u32[]{:S(2)}) collective-permute-start(bf16[64,512]{1,0:T(8,128)(2,1)S(1)} %fusion.2.refs_0_), channel_id=1, source_target_pairs={{0,8},{4,12},{8,0},{12,4},{1,9},{5,13},{9,1},{13,5},{2,10},{6,14},... | collective-permute-start | bytes 196616 | tf_op jit(solution)/shard_map/ppermute | solution.py:382
  59.5 9.9 %collective-permute-start.6 = (bf16[2,1088,128]{2,1,0:T(8,128)(2,1)S(1)}, bf16[2,1088,128]{2,1,0:T(8,128)(2,1)S(1)}, u32[]{:S(2)}, u32[]{:S(2)}) collective-permute-start(bf16[2,1088,128]{2,1,0:T(8,128)(2,1)S(1)} %copy-done.9), channel_id=1, source_target_pairs={{0,1},{1,0},{2,3},{3,2},{4,5},{5,4},{6,7},{7,6},{8,9},{9,8},{10,11... | collective-permute-start | bytes 1671176 | tf_op jit(solution)/shard_map/ppermute | solution.py:377
  59.5 20.2 %collective-permute-start.17 = (bf16[64,512]{1,0:T(8,128)(2,1)S(1)}, bf16[64,512]{1,0:T(8,128)(2,1)S(1)}, u32[]{:S(2)}, u32[]{:S(2)}) collective-permute-start(bf16[64,512]{1,0:T(8,128)(2,1)S(1)} %fusion.2.refs_0_), channel_id=1, source_target_pairs={{0,12},{4,0},{8,4},{12,8},{1,13},{5,1},{9,5},{13,9},{2,14},{6,2},{... | collective-permute-start | bytes 196616 | tf_op jit(solution)/shard_map/ppermute | solution.py:382
  64.7 15.2 %collective-permute-start.18 = (bf16[64,512]{1,0:T(8,128)(2,1)S(1)}, bf16[64,512]{1,0:T(8,128)(2,1)S(1)}, u32[]{:S(2)}, u32[]{:S(2)}) collective-permute-start(bf16[64,512]{1,0:T(8,128)(2,1)S(1)} %fusion.2.refs_0_), channel_id=1, source_target_pairs={{0,16},{16,0},{1,17},{17,1},{2,18},{18,2},{3,19},{19,3},{4,20},{20... | collective-permute-start | bytes 196616 | tf_op jit(solution)/shard_map/ppermute | solution.py:377
  66.2 16.9 %collective-permute-start.19 = (bf16[64,512]{1,0:T(8,128)(2,1)S(1)}, bf16[64,512]{1,0:T(8,128)(2,1)S(1)}, u32[]{:S(2)}, u32[]{:S(2)}) collective-permute-start(bf16[64,512]{1,0:T(8,128)(2,1)S(1)} %collective-permute-done.15.refs_1_), channel_id=1, source_target_pairs={{0,16},{16,0},{1,17},{17,1},{2,18},{18,2},{3,19},{19,3},{4,20},{20... | collective-permute-start | bytes 196616 | tf_op jit(solution)/shard_map/ppermute | solution.py:377
  66.7 17.0 %collective-permute-start.20 = (bf16[64,512]{1,0:T(8,128)(2,1)S(1)}, bf16[64,512]{1,0:T(8,128)(2,1)S(1)}, u32[]{:S(2)}, u32[]{:S(2)}) collective-permute-start(bf16[64,512]{1,0:T(8,128)(2,1)S(1)} %collective-permute-done.16.refs_2_), channel_id=1, source_target_pairs={{0,16},{16,0},{1,17},{17,1},{2,18},{18,2},{3,19},{19,3},{4,20},{20... | collective-permute-start | bytes 196616 | tf_op jit(solution)/shard_map/ppermute | solution.py:377
  69.6 8.3 %collective-permute-start.7 = (bf16[1,1088,128]{2,1,0:T(8,128)(2,1)S(1)}, bf16[1,1088,128]{2,1,0:T(8,128)(2,1)S(1)}, u32[]{:S(2)}, u32[]{:S(2)}) collective-permute-start(bf16[1,1088,128]{2,1,0:T(8,128)(2,1)S(1)} %slice.47), channel_id=1, source_target_pairs={{0,2},{1,3},{2,0},{3,1},{4,6},{5,7},{6,4},{7,5},{8,10},{9,11},{10,... | collective-permute-start | bytes 835592 | tf_op jit(solution)/shard_map/ppermute | solution.py:377
  77.9 7.0 %copy-start.11 = (s32[1,4,2]{1,2,0:T(2,128)S(1)}, s32[1,4,2]{1,2,0:T(2,128)}, u32[]{:S(2)}) copy-start(s32[1,4,2]{1,2,0:T(2,128)} %param.15) | copy-start | bytes 100
  77.9 11.7 %collective-permute-start.5 = (bf16[1,1040,128]{2,1,0:T(8,128)(2,1)S(1)}, bf16[1,1040,128]{2,1,0:T(8,128)(2,1)S(1)}, u32[]{:S(2)}, u32[]{:S(2)}) collective-permute-start(bf16[1,1040,128]{2,1,0:T(8,128)(2,1)S(1)} %get-tuple-element.30), channel_id=1, source_target_pairs={{0,2},{1,3},{2,0},{3,1},{4,6},{5,7},{6,4},{7,5},{8,10},{9,11},{10,... | collective-permute-start | bytes 798728 | tf_op jit(solution)/shard_map/ppermute | solution.py:377
  79.8 9.9 %collective-permute-start.10 = (bf16[544,128]{1,0:T(8,128)(2,1)S(1)}, bf16[544,128]{1,0:T(8,128)(2,1)S(1)}, u32[]{:S(2)}, u32[]{:S(2)}) collective-permute-start(bf16[544,128]{1,0:T(8,128)(2,1)S(1)} %slice_bitcast_fusion.1), channel_id=1, source_target_pairs={{0,8},{4,12},{8,0},{12,4},{1,9},{5,13},{9,1},{13,5},{2,10},{6,14},... | collective-permute-start | bytes 417800 | tf_op jit(solution)/shard_map/ppermute | solution.py:382
  79.9 9.8 %collective-permute-start.8 = (bf16[272,128]{1,0:T(8,128)(2,1)S(1)}, bf16[272,128]{1,0:T(8,128)(2,1)S(1)}, u32[]{:S(2)}, u32[]{:S(2)}) collective-permute-start(bf16[272,128]{1,0:T(8,128)(2,1)S(1)} %get-tuple-element.33), channel_id=1, source_target_pairs={{0,12},{4,0},{8,4},{12,8},{1,13},{5,1},{9,5},{13,9},{2,14},{6,2},{... | collective-permute-start | bytes 208904 | tf_op jit(solution)/shard_map/ppermute | solution.py:382
  83.1 6.5 %collective-permute-start.9 = (bf16[272,128]{1,0:T(8,128)(2,1)S(1)}, bf16[272,128]{1,0:T(8,128)(2,1)S(1)}, u32[]{:S(2)}, u32[]{:S(2)}) collective-permute-start(bf16[272,128]{1,0:T(8,128)(2,1)S(1)} %get-tuple-element.32), channel_id=1, source_target_pairs={{0,4},{4,8},{8,12},{12,0},{1,5},{5,9},{9,13},{13,1},{2,6},{6,10},{... | collective-permute-start | bytes 208904 | tf_op jit(solution)/shard_map/ppermute | solution.py:382
  83.7 4.3 %collective-permute-start.21 = (bf16[64,512]{1,0:T(8,128)(2,1)S(1)}, bf16[64,512]{1,0:T(8,128)(2,1)S(1)}, u32[]{:S(2)}, u32[]{:S(2)}) collective-permute-start(bf16[64,512]{1,0:T(8,128)(2,1)S(1)} %collective-permute-done.17.refs_3_), channel_id=1, source_target_pairs={{0,16},{16,0},{1,17},{17,1},{2,18},{18,2},{3,19},{19,3},{4,20},{20... | collective-permute-start | bytes 196616 | tf_op jit(solution)/shard_map/ppermute | solution.py:377
  (2 other events, 1.6 us)
